TPU v7x, 128 devices: a whole 4x4x4 slice. The times are simulated.
128 devices in a mesh: row: 4 (over z_hi, core), tm: 32 (over y, z_lo, x).
Axes of the slice: x: 4, y: 4, z: 4 (z_hi: 2, z_lo: 2; z = z_hi * 2 + z_lo), core: 2. Of those that a mesh axis runs over, the one named last changes fastest.
Arguments:
- temps: bfloat16 [24576, 16384], P('row', 'tm')
- area: float32 [24576], P('row'), may hold values from 0.2 to 1
- ocean_rows: int32 [24576], P('row'), may hold values from 0 to 6143, as said below
- counts: int32 [4], P('row'), may hold values from 1536 to 6144, as said below
Outputs:
- band: float32 [2048, 16384], P('row', 'tm')
Inputs may be any that keep to these rules, and one draw needn't show every extreme that they name: `ocean_rows`: within each tile of 6144 entries, every local row number appears once. `counts`: some tile is all ocean.
All inputs are finite; a program needn't handle non-finite values.
Results may differ from a plain program's by a relative error of at most 0.0022.
Values may be sent and summed in bfloat16 or wider, within the bound.
A program may use at most 64 MiB of HBM per device.

v0:
```python
import jax
import jax.numpy as jnp
from jax import lax
from jax.sharding import PartitionSpec as P

LAGS = 4


def shifted(value, axis, steps):
    count = lax.axis_size(axis)
    pairs = [(source, (source + steps) % count) for source in range(count)]
    return lax.ppermute(value, axis, pairs)


def body(temps, area, ocean_rows, counts):
    rows, hours = temps.shape
    total_hours = hours * lax.axis_size("tm")
    total_rows = rows * lax.axis_size("row")
    sums = jnp.sum(temps, axis=1, dtype=jnp.float32)
    mean = lax.psum(sums, "tm") / total_hours
    live = (jnp.arange(rows, dtype=jnp.int32) < counts[0]).astype(jnp.float32)
    ocean = jnp.zeros((rows,), jnp.float32).at[ocean_rows].set(live)
    weighted = ((temps.astype(jnp.float32) - mean[:, None]) * (ocean * area)[:, None]).astype(
        jnp.bfloat16
    )
    others = [weighted]
    current = weighted
    for lag in range(1, LAGS):
        current = shifted(current, "tm", -1)
        others.append(current)
    joined = jnp.concatenate(others, axis=1)
    contract = (((0,), (0,)), ((), ()))
    terms = lax.dot_general(joined, weighted, contract, preferred_element_type=jnp.float32)
    summed = lax.psum_scatter(terms, "row", scatter_dimension=0, tiled=True)
    return summed / jnp.sqrt(jnp.float32(total_rows))


def solution(mesh):
    in_specs = (P("row", "tm"), P("row"), P("row"), P("row"))
    out_specs = P("row", "tm")
    return jax.shard_map(body, mesh=mesh, in_specs=in_specs, out_specs=out_specs, check_vma=False)
```

profile of v0, /device:TPU:1, one launch (start us, length us, event | category | flops | bytes accessed | tf_op | source)
XLA Modules:
  0.0 656.1 jit_solution(8619647536048842335)
XLA Ops:
  6.5 0.0 copy-start
  6.5 0.0 reduce-scatter.2.cloned.1.call-start
  7.2 0.7 compare_select_fusion
  8.0 3.7 convert_reduce_fusion
  11.7 131.5 %psum.7 = f32[6144]{0:T(1024)S(1)} all-reduce(f32[6144]{0:T(1024)S(1)} %convert_reduce_fusion), channel_id=1, replica_groups=mesh['row'=4,'tm'=32] {'tm'}, use_global_device_ids=true, to_apply=%region_1.0 | all-reduce | flops 6144 | bytes 49152 | tf_op jit(solution)/shard_map/psum | solution.py:20
  143.1 23.0 %scatter_custom_fusion = f32[6144]{0:T(1024)S(1)} fusion(s32[6144]{0:T(1024)S(1)} %compare_select_fusion, f32[6144]{0:T(1024)S(1)} %fusion.10, f32[]{:T(128)} %constant.5.clone.1), kind=kCustom, calls=%fused_computation.17 | custom fusion | bytes 24580 | tf_op jit(solution)/shard_map/scatter | solution.py:22
  166.2 0.0 copy-done
  166.2 4.4 fusion.9
  170.6 0.1 collective-permute-start
  170.7 108.4 %collective-permute-done = bf16[6144,512]{1,0:T(8,128)(2,1)S(1)} collective-permute-done((bf16[6144,512]{1,0:T(8,128)(2,1)S(1)}, bf16[6144,512]{1,0:T(8,128)(2,1)S(1)}, u32[]{:S(2)}, u32[]{:S(2)}) %collective-permute-start) | collective-permute-done | bytes 6291488 | tf_op jit(solution)/shard_map/ppermute | solution.py:12
  279.1 4.5 collective-permute-start.1
  283.6 129.5 %collective-permute-done.1 = bf16[6144,512]{1,0:T(8,128)(2,1)S(1)} collective-permute-done((bf16[6144,512]{1,0:T(8,128)(2,1)S(1)}, bf16[6144,512]{1,0:T(8,128)(2,1)S(1)}, u32[]{:S(2)}, u32[]{:S(2)}) %collective-permute-start.1) | collective-permute-done | bytes 6291488 | tf_op jit(solution)/shard_map/ppermute | solution.py:12
  413.0 4.5 collective-permute-start.2
  417.6 129.6 %collective-permute-done.2 = bf16[6144,512]{1,0:T(8,128)(2,1)} collective-permute-done((bf16[6144,512]{1,0:T(8,128)(2,1)S(1)}, bf16[6144,512]{1,0:T(8,128)(2,1)}, u32[]{:S(2)}, u32[]{:S(2)}) %collective-permute-start.2) | collective-permute-done | bytes 6291488 | tf_op jit(solution)/shard_map/ppermute | solution.py:12
  547.1 17.6 %fusion = f32[2048,512]{1,0:T(8,128)} fusion(bf16[6144,512]{1,0:T(8,128)(2,1)S(1)} %fusion.9, bf16[6144,512]{1,0:T(8,128)(2,1)} %collective-permute-done.2, bf16[6144,512]{1,0:T(8,128)(2,1)S(1)} %collective-permute-done.1, bf16[6144,512]{1,0:T(8,128)(2,1)S(1)} %collective-permute-done), kind=kOutput, calls=%fused_computation.1 | convolution fusion | flops 12985565184 | bytes 29360128 | tf_op jit(solution)/shard_map/dot_general | solution.py:33
  564.7 0.0 reduce-scatter.2.cloned.1.call-update
  564.8 82.2 %reduce-scatter.2.cloned.1.call-done = f32[512,512]{1,0:T(8,128)} async-done(((f32[2048,512]{1,0:T(8,128)}), f32[512,512]{1,0:T(8,128)}) %reduce-scatter.2.cloned.1.call-update) | async-done | bytes 1048592 | tf_op jit(solution)/shard_map/reduce_scatter | solution.py:34
  646.9 2.3 broadcast_multiply_fusion
  (3 shorter events, 0.0 us)
Async XLA Ops:
  6.5 159.6 %copy-start = (f32[6144]{0:T(1024)S(1)}, f32[6144]{0:T(1024)}, u32[]{:S(2)}) copy-start(f32[6144]{0:T(1024)} %param.5) | copy-start | bytes 73732
  6.5 640.4 %reduce-scatter.2.cloned.1.call-start = ((), (), s32[]{:S(2)}) async-start(), calls=%async_computation.1 | async-start | bytes 5242880 | tf_op jit(solution)/shard_map/reduce_scatter | solution.py:34
  170.6 108.4 %collective-permute-start = (bf16[6144,512]{1,0:T(8,128)(2,1)S(1)}, bf16[6144,512]{1,0:T(8,128)(2,1)S(1)}, u32[]{:S(2)}, u32[]{:S(2)}) collective-permute-start(bf16[6144,512]{1,0:T(8,128)(2,1)S(1)} %fusion.9), channel_id=1, source_target_pairs={{0,31},{1,0},{2,1},{3,2},{4,3},{5,4},{6,5},{7,6},{8,7},{9,8},{10,9... | collective-permute-start | bytes 18874376 | tf_op jit(solution)/shard_map/ppermute | solution.py:12
  279.1 134.0 %collective-permute-start.1 = (bf16[6144,512]{1,0:T(8,128)(2,1)S(1)}, bf16[6144,512]{1,0:T(8,128)(2,1)S(1)}, u32[]{:S(2)}, u32[]{:S(2)}) collective-permute-start(bf16[6144,512]{1,0:T(8,128)(2,1)S(1)} %collective-permute-done), channel_id=1, source_target_pairs={{0,31},{1,0},{2,1},{3,2},{4,3},{5,4},{6,5},{7,6},{8,7},{9,8},{10,9... | collective-permute-start | bytes 18874376 | tf_op jit(solution)/shard_map/ppermute | solution.py:12
  413.0 134.1 %collective-permute-start.2 = (bf16[6144,512]{1,0:T(8,128)(2,1)S(1)}, bf16[6144,512]{1,0:T(8,128)(2,1)}, u32[]{:S(2)}, u32[]{:S(2)}) collective-permute-start(bf16[6144,512]{1,0:T(8,128)(2,1)S(1)} %collective-permute-done.1), channel_id=1, source_target_pairs={{0,31},{1,0},{2,1},{3,2},{4,3},{5,4},{6,5},{7,6},{8,7},{9,8},{10,9... | collective-permute-start | bytes 18874376 | tf_op jit(solution)/shard_map/ppermute | solution.py:12
Sparse Core Ops, SparseCore 0:
  564.9 82.0 reduce-scatter.1
where the time goes:
time: 656 us
  waiting for transfers between devices  450 us (69%)
  blocking collectives  131 us (20%)
  local copies, waits for them, and re-layouts  23 us (4%)
  matrix products  17.6 us (3%)
  between operations  14.1 us (2%)
  other arithmetic  11.2 us (2%)
  starting transfers between devices  9.09 us (1%)
    ppermute x3, waiting for transfers between devices, shifted(): return lax.ppermute(value, axis, pairs)  367 us
    psum x1, blocking collectives, body(): mean = lax.psum(sums, 'tm') / total_hours  131 us
    reduce_scatter x1, waiting for transfers between devices, body(): summed = lax.psum_scatter(terms, 'row', scatter_dimension=0, tiled=True)  82.2 us
    scatter x1, local copies, waits for them, and re-layouts, body(): ocean = jnp.zeros((rows,), jnp.float32).at[ocean_rows].set(live)  23 us
    dot_general x1, matrix products, body(): lax.dot_general(joined, weighted, contract, preferred_element_type=jnp.fl...  17.6 us
  transfers between devices with their start and end apart: 4, of which 4 were waited for; matrix products, arithmetic and copies ran while one was open for 0% of the time, Pallas kernels for 0%

commit v1 on v0

--- a/solution.py
+++ b/solution.py
@@ -17,7 +17,7 @@
     total_hours = hours * lax.axis_size("tm")
     total_rows = rows * lax.axis_size("row")
     sums = jnp.sum(temps, axis=1, dtype=jnp.float32)
-    mean = lax.psum(sums, "tm") / total_hours
+    mean = jnp.sum(lax.all_gather(sums, "tm"), axis=0) / total_hours
     live = (jnp.arange(rows, dtype=jnp.int32) < counts[0]).astype(jnp.float32)
     ocean = jnp.zeros((rows,), jnp.float32).at[ocean_rows].set(live)
     weighted = ((temps.astype(jnp.float32) - mean[:, None]) * (ocean * area)[:, None]).astype(

time: 656 us -> 598 us (0.912)
  blocking collectives: 131 us -> 73.2 us
    psum x1 -> x0, blocking collectives: 131 us -> none  [body(): mean = lax.psum(sums, 'tm') / total_hours]
    all_gather x0 -> x1, blocking collectives: none -> 73.2 us  [body(): mean = jnp.sum(lax.all_gather(sums, 'tm'), axis=0) / total_hours]
    reduce_scatter x1, waiting for transfers between devices: 82.2 us -> 68 us  [body(): summed = lax.psum_scatter(terms, 'row', scatter_dimension=0, tiled=True)]
    ppermute x3, waiting for transfers between devices: 367 us -> 382 us  [shifted(): return lax.ppermute(value, axis, pairs)]
where the time goes in v1:
time: 598 us
  waiting for transfers between devices  450 us (75%)
  blocking collectives  73.2 us (12%)
  local copies, waits for them, and re-layouts  23.1 us (4%)
  matrix products  17.6 us (3%)
  between operations  14.1 us (2%)
  other arithmetic  11.3 us (2%)
  starting transfers between devices  9.09 us (2%)
    ppermute x3, waiting for transfers between devices, shifted(): return lax.ppermute(value, axis, pairs)  382 us
    all_gather x1, blocking collectives, body(): mean = jnp.sum(lax.all_gather(sums, 'tm'), axis=0) / total_hours  73.2 us
    reduce_scatter x1, waiting for transfers between devices, body(): summed = lax.psum_scatter(terms, 'row', scatter_dimension=0, tiled=True)  68 us
    scatter x1, local copies, waits for them, and re-layouts, body(): ocean = jnp.zeros((rows,), jnp.float32).at[ocean_rows].set(live)  23 us
    dot_general x1, matrix products, body(): lax.dot_general(joined, weighted, contract, preferred_element_type=jnp.fl...  17.6 us
  transfers between devices with their start and end apart: 4, of which 4 were waited for; matrix products, arithmetic and copies ran while one was open for 0% of the time, Pallas kernels for 0%

profile of v1, /device:TPU:1, one launch (start us, length us, event | category | flops | bytes accessed | tf_op | source)
XLA Modules:
  0.0 598.0 jit_solution(8742997095590576500)
XLA Ops:
  6.5 0.0 copy-start
  6.5 0.0 reduce-scatter.2.cloned.1.call-start
  7.2 0.7 compare_select_fusion
  8.0 3.7 convert_reduce_fusion
  11.7 73.2 %all-gather = f32[196608]{0:T(1024)S(1)} all-gather(f32[6144]{0:T(1024)S(1)} %convert_reduce_fusion), channel_id=2, replica_groups=mesh['row'=4,'tm'=32] {'tm'}, dimensions={0}, use_global_device_ids=true | all-gather | bytes 811008 | tf_op jit(solution)/shard_map/all_gather | solution.py:20
  84.8 0.1 reshape.12
  85.0 0.1 reduce_sum.19
  85.0 23.0 %scatter_custom_fusion = f32[6144]{0:T(1024)S(1)} fusion(s32[6144]{0:T(1024)S(1)} %compare_select_fusion, f32[6144]{0:T(1024)S(1)} %fusion.10, f32[]{:T(128)} %constant.5.clone.1), kind=kCustom, calls=%fused_computation.17 | custom fusion | bytes 24580 | tf_op jit(solution)/shard_map/scatter | solution.py:22
  108.1 0.0 copy-done
  108.1 4.4 fusion.9
  112.5 0.1 collective-permute-start
  112.6 122.5 %collective-permute-done = bf16[6144,512]{1,0:T(8,128)(2,1)S(1)} collective-permute-done((bf16[6144,512]{1,0:T(8,128)(2,1)S(1)}, bf16[6144,512]{1,0:T(8,128)(2,1)S(1)}, u32[]{:S(2)}, u32[]{:S(2)}) %collective-permute-start) | collective-permute-done | bytes 6291488 | tf_op jit(solution)/shard_map/ppermute | solution.py:12
  235.1 4.5 collective-permute-start.1
  239.6 129.5 %collective-permute-done.1 = bf16[6144,512]{1,0:T(8,128)(2,1)S(1)} collective-permute-done((bf16[6144,512]{1,0:T(8,128)(2,1)S(1)}, bf16[6144,512]{1,0:T(8,128)(2,1)S(1)}, u32[]{:S(2)}, u32[]{:S(2)}) %collective-permute-start.1) | collective-permute-done | bytes 6291488 | tf_op jit(solution)/shard_map/ppermute | solution.py:12
  369.1 4.5 collective-permute-start.2
  373.6 129.6 %collective-permute-done.2 = bf16[6144,512]{1,0:T(8,128)(2,1)} collective-permute-done((bf16[6144,512]{1,0:T(8,128)(2,1)S(1)}, bf16[6144,512]{1,0:T(8,128)(2,1)}, u32[]{:S(2)}, u32[]{:S(2)}) %collective-permute-start.2) | collective-permute-done | bytes 6291488 | tf_op jit(solution)/shard_map/ppermute | solution.py:12
  503.2 17.6 %fusion = f32[2048,512]{1,0:T(8,128)} fusion(bf16[6144,512]{1,0:T(8,128)(2,1)S(1)} %fusion.9, bf16[6144,512]{1,0:T(8,128)(2,1)} %collective-permute-done.2, bf16[6144,512]{1,0:T(8,128)(2,1)S(1)} %collective-permute-done.1, bf16[6144,512]{1,0:T(8,128)(2,1)S(1)} %collective-permute-done), kind=kOutput, calls=%fused_computation.1 | convolution fusion | flops 12985565184 | bytes 29360128 | tf_op jit(solution)/shard_map/dot_general | solution.py:33
  520.8 0.0 reduce-scatter.2.cloned.1.call-update
  520.8 68.0 %reduce-scatter.2.cloned.1.call-done = f32[512,512]{1,0:T(8,128)} async-done(((f32[2048,512]{1,0:T(8,128)}), f32[512,512]{1,0:T(8,128)}) %reduce-scatter.2.cloned.1.call-update) | async-done | bytes 1048592 | tf_op jit(solution)/shard_map/reduce_scatter | solution.py:34
  588.8 2.3 broadcast_multiply_fusion
  (3 shorter events, 0.0 us)
Async XLA Ops:
  6.5 101.5 %copy-start = (f32[6144]{0:T(1024)S(1)}, f32[6144]{0:T(1024)}, u32[]{:S(2)}) copy-start(f32[6144]{0:T(1024)} %param.5) | copy-start | bytes 73732
  6.5 582.3 %reduce-scatter.2.cloned.1.call-start = ((), (), s32[]{:S(2)}) async-start(), calls=%async_computation.1 | async-start | bytes 5242880 | tf_op jit(solution)/shard_map/reduce_scatter | solution.py:34
  112.5 122.6 %collective-permute-start = (bf16[6144,512]{1,0:T(8,128)(2,1)S(1)}, bf16[6144,512]{1,0:T(8,128)(2,1)S(1)}, u32[]{:S(2)}, u32[]{:S(2)}) collective-permute-start(bf16[6144,512]{1,0:T(8,128)(2,1)S(1)} %fusion.9), channel_id=1, source_target_pairs={{0,31},{1,0},{2,1},{3,2},{4,3},{5,4},{6,5},{7,6},{8,7},{9,8},{10,9... | collective-permute-start | bytes 18874376 | tf_op jit(solution)/shard_map/ppermute | solution.py:12
  235.1 134.0 %collective-permute-start.1 = (bf16[6144,512]{1,0:T(8,128)(2,1)S(1)}, bf16[6144,512]{1,0:T(8,128)(2,1)S(1)}, u32[]{:S(2)}, u32[]{:S(2)}) collective-permute-start(bf16[6144,512]{1,0:T(8,128)(2,1)S(1)} %collective-permute-done), channel_id=1, source_target_pairs={{0,31},{1,0},{2,1},{3,2},{4,3},{5,4},{6,5},{7,6},{8,7},{9,8},{10,9... | collective-permute-start | bytes 18874376 | tf_op jit(solution)/shard_map/ppermute | solution.py:12
  369.1 134.1 %collective-permute-start.2 = (bf16[6144,512]{1,0:T(8,128)(2,1)S(1)}, bf16[6144,512]{1,0:T(8,128)(2,1)}, u32[]{:S(2)}, u32[]{:S(2)}) collective-permute-start(bf16[6144,512]{1,0:T(8,128)(2,1)S(1)} %collective-permute-done.1), channel_id=1, source_target_pairs={{0,31},{1,0},{2,1},{3,2},{4,3},{5,4},{6,5},{7,6},{8,7},{9,8},{10,9... | collective-permute-start | bytes 18874376 | tf_op jit(solution)/shard_map/ppermute | solution.py:12
Sparse Core Ops, SparseCore 0:
  520.9 67.8 reduce-scatter.1
